TPU v7x, 512 devices: a whole 4x4x16 slice. The times are simulated.
512 devices in a mesh: ctx: 32 (over x_lo, z), tp: 16 (over x_hi, y, core).
Axes of the slice: x: 4 (x_hi: 2, x_lo: 2; x = x_hi * 2 + x_lo), y: 4, z: 16, core: 2. Of those that a mesh axis runs over, the one named last changes fastest.
Arguments:
- queries: bfloat16 [512, 128, 576], P('ctx', 'tp'), may hold values from -90 to 90
- grad_out: bfloat16 [512, 128, 512], P('ctx', 'tp'), may hold values from -6 to 6
- latent_cache: bfloat16 [4096, 576], P('ctx'), may hold values from -6 to 6
- slab_starts: int32 [32], P('ctx'), may hold values from 0 to 4080, as said below
Outputs:
- query_grad: bfloat16 [512, 128, 576], P('ctx', 'tp')
- cache_grad: float32 [4096, 576], P('ctx')
Inputs may be any that keep to these rules, and one draw needn't show every extreme that they name: `slab_starts`: some slab starts at 0 and some at 4080.
All inputs are finite; a program needn't handle non-finite values.
Results may differ from a plain program's by a relative error of at most 0.0049.
Values may be sent and summed in bfloat16 or wider, within the bound.
A program may use at most 64 MiB of HBM per device.

v0:
```python
import jax
import jax.numpy as jnp
from jax import lax
from jax.sharding import PartitionSpec as P

ROPE = 64
NOPE = 128


def masked_scores(rows_query, key_block, row_pos, key_pos, score_scale):
    raw = (
        jnp.einsum("rd,kd->rk", rows_query, key_block, preferred_element_type=jnp.float32)
        * score_scale
    )
    return jnp.where(key_pos[None, :] <= row_pos[:, None], raw, -jnp.inf)


def on_device(queries, grad_out, latent_cache, slab_starts):
    slab_len, head_local, full_width = queries.shape
    latent_width = grad_out.shape[2]
    cache_len = latent_cache.shape[0]
    score_scale = (NOPE + ROPE) ** (-0.5)
    ctx_count = lax.axis_size("ctx")
    rows_local = slab_len * head_local
    rows_query = queries.reshape(rows_local, full_width)
    rows_cotan = grad_out.reshape(rows_local, latent_width)
    row_pos = jnp.repeat(slab_starts[0] + jnp.arange(slab_len, dtype=jnp.int32), head_local)
    start_table = lax.all_gather(slab_starts, "ctx", axis=0, tiled=True)
    gathered = lax.all_gather(latent_cache, "ctx", axis=0, tiled=True)
    key_pos = jnp.arange(ctx_count * cache_len, dtype=jnp.int32)
    seq_len = gathered.shape[0]
    block_len = min(512, seq_len)
    block_count = seq_len // block_len
    key_blocks = gathered.reshape(block_count, block_len, full_width)
    pos_blocks = key_pos.reshape(block_count, block_len)

    def stats_step(state_now, block_item):
        key_block, block_pos = block_item
        running_max, running_sum, running_dot = state_now
        scores = masked_scores(rows_query, key_block, row_pos, block_pos, score_scale)
        grad_probs = jnp.einsum(
            "rd,kd->rk", rows_cotan, key_block[:, :latent_width], preferred_element_type=jnp.float32
        )
        new_max = jnp.maximum(running_max, jnp.max(scores, axis=1))
        shrink = jnp.exp(running_max - new_max)
        probs = jnp.exp(scores - new_max[:, None])
        state_out = (
            new_max,
            running_sum * shrink + jnp.sum(probs, axis=1),
            running_dot * shrink + jnp.sum(probs * grad_probs, axis=1),
        )
        return (state_out, None)

    first_state = (
        jnp.full((rows_local,), -1e30, jnp.float32),
        jnp.zeros((rows_local,), jnp.float32),
        jnp.zeros((rows_local,), jnp.float32),
    )
    (running_max, running_sum, running_dot), _ = lax.scan(
        stats_step, first_state, (key_blocks, pos_blocks)
    )
    log_total = running_max + jnp.log(running_sum)
    row_delta = running_dot / running_sum

    def grad_step(grad_acc, block_item):
        key_block, block_pos = block_item
        scores = masked_scores(rows_query, key_block, row_pos, block_pos, score_scale)
        grad_probs = jnp.einsum(
            "rd,kd->rk", rows_cotan, key_block[:, :latent_width], preferred_element_type=jnp.float32
        )
        probs = jnp.exp(scores - log_total[:, None])
        grad_scores = (probs * (grad_probs - row_delta[:, None])).astype(jnp.bfloat16)
        acc_out = grad_acc + jnp.dot(grad_scores, key_block, preferred_element_type=jnp.float32)
        return (acc_out, None)

    grad_acc, _ = lax.scan(
        grad_step, jnp.zeros((rows_local, full_width), jnp.float32), (key_blocks, pos_blocks)
    )
    query_grad = (
        (score_scale * grad_acc).astype(jnp.bfloat16).reshape(slab_len, head_local, full_width)
    )
    total_all, delta_all = (
        lax.all_gather(log_total, "ctx", axis=0, tiled=True),
        lax.all_gather(row_delta, "ctx", axis=0, tiled=True),
    )
    own_pos = lax.axis_index("ctx") * cache_len + jnp.arange(cache_len, dtype=jnp.int32)
    value_cols = latent_cache[:, :latent_width]
    slab_ids = jnp.arange(ctx_count, dtype=jnp.int32)
    piece_query = lax.all_gather(rows_query, "ctx", axis=0, tiled=True)
    piece_cotan = lax.all_gather(rows_cotan, "ctx", axis=0, tiled=True)
    piece_len = piece_query.shape[0]
    row_index = jnp.arange(piece_len, dtype=jnp.int32)
    row_slab = row_index // rows_local
    row_query = row_index % rows_local // head_local
    slab_first = jnp.sum(
        jnp.where(row_slab[:, None] == slab_ids[None, :], start_table[None, :], 0), axis=1
    )
    piece_pos = slab_first + row_query
    scores = masked_scores(piece_query, latent_cache, piece_pos, own_pos, score_scale)
    grad_probs = jnp.einsum(
        "rd,kd->rk", piece_cotan, value_cols, preferred_element_type=jnp.float32
    )
    probs = jnp.exp(scores - total_all[:, None])
    grad_scores = (probs * (grad_probs - delta_all[:, None])).astype(jnp.bfloat16)
    probs_low = probs.astype(jnp.bfloat16)
    score_part = jnp.einsum(
        "rk,rd->kd", grad_scores, piece_query, preferred_element_type=jnp.float32
    )
    value_part = jnp.einsum("rk,rd->kd", probs_low, piece_cotan, preferred_element_type=jnp.float32)
    score_part, value_part = (score_part, value_part)
    local_grad = score_scale * score_part + jnp.pad(
        value_part, ((0, 0), (0, full_width - latent_width))
    )
    cache_grad = lax.psum(local_grad, "tp")
    return (query_grad, cache_grad)


def solution(mesh):
    placed = (P("ctx", "tp", None), P("ctx", "tp", None), P("ctx", None), P("ctx"))
    return jax.shard_map(
        on_device,
        mesh=mesh,
        in_specs=placed,
        out_specs=(P("ctx", "tp", None), P("ctx", None)),
        check_vma=False,
    )
```

profile of v0, /device:TPU:1, one launch (start us, length us, event | category | flops | bytes accessed | tf_op | source)
XLA Modules:
  0.0 595.3 jit_solution(4402013973316383230)
XLA Ops:
  10.2 1.3 dynamic-slice
  12.2 26.8 %all-reduce.1 = s32[32]{0:T(128)S(1)} all-reduce(s32[32]{0:T(128)S(1)} %dynamic-update-slice), channel_id=1, replica_groups=mesh['ctx'=32,'tp'=16] {'ctx'}, use_global_device_ids=true, to_apply=%add.1 | all-reduce | flops 32 | bytes 256
  39.2 101.6 %all-gather.6.cloned.1.call-done = bf16[4096,576]{0,1:T(8,128)(2,1)} async-done(((bf16[128,576]{0,1:T(8,128)(2,1)}), bf16[4096,576]{0,1:T(8,128)(2,1)}) %all-gather.6.cloned.1.call-update) | async-done | bytes 4718608 | tf_op jit(solution)/shard_map/all_gather | solution.py:29
  140.8 7.6 %copy.15 = bf16[4096,576]{1,0:T(8,128)(2,1)} copy(bf16[4096,576]{0,1:T(8,128)(2,1)} %all-gather.6.cloned.1.call-done) | data formatting | bytes 9437184 | tf_op jit(solution)/shard_map/all_gather | solution.py:29
  148.5 17.2 %while.26 = (s32[]{:T(128)}, f32[128]{0:T(128)S(1)}, f32[128]{0:T(128)S(1)}, f32[128]{0:T(128)S(1)}, s32[8,512]{1,0:T(8,128)S(1)}, /*index=5*/bf16[8,512,576]{2,...) while((s32[]{:T(128)}, f32[128]{0:T(128)S(1)}, ...), condition=%wide.region_4.5_spmd.clone, body=%wide.region_0.4_spmd.clone.sunk | while | flops 143197056 | bytes 3376328 | solution.py:59
  148.5 1.2 dynamic-slice_bitcast_fusion.4
  150.7 1.1 dynamic-slice_bitcast_fusion.4
  152.8 1.1 dynamic-slice_bitcast_fusion.4
  155.0 1.1 dynamic-slice_bitcast_fusion.4
  157.1 1.1 dynamic-slice_bitcast_fusion.4
  159.2 1.1 dynamic-slice_bitcast_fusion.4
  161.4 1.1 dynamic-slice_bitcast_fusion.4
  163.5 1.1 dynamic-slice_bitcast_fusion.4
  165.7 48.4 %all-gather = f32[32,1,128]{2,1,0:T(1,128)S(1)} all-gather(f32[1,1,128]{2,1,0:T(1,128)S(1)} %bitcast.92), channel_id=1, replica_groups=mesh['ctx'=32,'tp'=16] {'ctx'}, dimensions={0}, use_global_device_ids=true | all-gather | bytes 16896 | tf_op jit(solution)/shard_map/all_gather | solution.py:83
  214.1 46.0 %all-gather.1 = f32[32,1,128]{2,1,0:T(1,128)S(1)} all-gather(f32[1,1,128]{2,1,0:T(1,128)S(1)} %bitcast.93), channel_id=1, replica_groups=mesh['ctx'=32,'tp'=16] {'ctx'}, dimensions={0}, use_global_device_ids=true | all-gather | bytes 16896 | tf_op jit(solution)/shard_map/all_gather | solution.py:84
  260.0 22.5 %all-gather.8.cloned.1.call-done = bf16[4096,576]{1,0:T(8,128)(2,1)} async-done(((bf16[128,576]{1,0:T(8,128)(2,1)}), bf16[4096,576]{1,0:T(8,128)(2,1)}) %all-gather.8.cloned.1.call-update) | async-done | bytes 4718608 | tf_op jit(solution)/shard_map/all_gather | solution.py:89
  282.5 5.7 fusion.28
  288.2 128.8 %all-gather.10.cloned.1.call-done = bf16[4096,512]{1,0:T(8,128)(2,1)} async-done(((bf16[128,512]{1,0:T(8,128)(2,1)}), bf16[4096,512]{1,0:T(8,128)(2,1)}) %all-gather.10.cloned.1.call-update) | async-done | bytes 4194320 | tf_op jit(solution)/shard_map/all_gather | solution.py:90
  417.0 3.9 fusion.31
  420.9 8.2 %fusion.30 = f32[128,576]{0,1:T(8,128)} fusion(bf16[4096,576]{1,0:T(8,128)(2,1)} %all-gather.8.cloned.1.call-done, f32[4096,128]{1,0:T(8,128)S(1)} %fusion.28, bf16[4096,512]{1,0:T(8,128)(2,1)} %all-gather.10.cloned.1.call-done, f32[4096]{0:T(1024)S(1)} %bitcast.91, f32[128,512]{0,1:T(8,128)S(1)} %fusion.31, bf16[128,576]{0,1:T(8,128)(2,1)S(1)} %copy-done.2), kind=kOutput, calls=%fused_computation.44 | convolution fusion | flops 1142571008 | bytes 11714560 | tf_op jit(solution)/shard_map/rk,rd->kd/dot_general | solution.py:106
  429.2 20.0 %while.27 = (s32[]{:T(128)}, f32[128,576]{0,1:T(8,128)S(1)}, s32[8,512]{1,0:T(8,128)S(1)}, bf16[8,512,576]{2,1,0:T(8,128)(2,1)}, bf16[128,576]{1,0:T(8,128)(2,1)...) while((s32[]{:T(128)}, f32[128,576]{0,1:T(8,128)S(1)}, ...), condition=%wide.region_6.7_spmd.clone, body=%wide.region_5.6_spmd.clone.sunk | while | flops 218710016 | bytes 4351175 | solution.py:76
  429.2 1.1 dynamic-slice_bitcast_fusion.5
  450.0 137.1 %all-reduce.4.cloned.1.call-done = f32[128,576]{0,1:T(8,128)} async-done(((f32[128,576]{0,1:T(8,128)}), f32[128,576]{0,1:T(8,128)}) %all-reduce.4.cloned.1.call-update) | async-done | bytes 294928 | tf_op jit(solution)/shard_map/psum | solution.py:114
  587.1 1.7 copy.40
  (148 shorter events, 30.0 us)
Async XLA Ops:
  7.2 133.7 %all-gather.6.cloned.1.call-start = ((), (), s32[]{:S(2)}) async-start(), calls=%async_computation | async-start | bytes 4866048 | tf_op jit(solution)/shard_map/all_gather | solution.py:29
  7.9 274.6 %all-gather.8.cloned.1.call-start = ((), (), s32[]{:S(2)}) async-start(), calls=%async_computation.1 | async-start | bytes 5406720 | tf_op jit(solution)/shard_map/all_gather | solution.py:89
  8.6 408.4 %all-gather.10.cloned.1.call-start = ((), (), s32[]{:S(2)}) async-start(), calls=%async_computation.2 | async-start | bytes 4325376 | tf_op jit(solution)/shard_map/all_gather | solution.py:90
  9.4 577.7 %all-reduce.4.cloned.1.call-start = ((), (), s32[]{:S(2)}) async-start(), calls=%async_computation.3 | async-start | bytes 589824 | tf_op jit(solution)/shard_map/psum | solution.py:114
  39.2 109.3 %copy-start = (bf16[16,8,576]{2,1,0:T(8,128)(2,1)S(1)}, bf16[16,8,576]{2,1,0:T(8,128)(2,1)}, u32[]{:S(2)}) copy-start(bf16[16,8,576]{2,1,0:T(8,128)(2,1)} %param.8) | copy-start | bytes 442372
  39.2 109.3 %copy-start.1 = (bf16[16,8,512]{2,1,0:T(8,128)(2,1)S(1)}, bf16[16,8,512]{2,1,0:T(8,128)(2,1)}, u32[]{:S(2)}) copy-start(bf16[16,8,512]{2,1,0:T(8,128)(2,1)} %param.9) | copy-start | bytes 393220
  148.5 134.0 %copy-start.2 = (bf16[128,576]{0,1:T(8,128)(2,1)S(1)}, bf16[128,576]{0,1:T(8,128)(2,1)}, u32[]{:S(2)}) copy-start(bf16[128,576]{0,1:T(8,128)(2,1)} %param.10) | copy-start | bytes 442372
Sparse Core Ops, SparseCore 0:
  10.0 130.7 all-gather.5
  142.9 139.5 all-gather.7
  284.6 132.3 all-gather.9
  429.3 157.7 all-reduce.3
where the time goes:
time: 598 us; the launch traced here: 595 us
  waiting for transfers between devices  392 us (66%)
  blocking collectives  121 us (20%)
  local copies, waits for them, and re-layouts  33.3 us (6%)
  matrix products  32.2 us (5%)
  between operations  14.6 us (2%)
    psum x1, waiting for transfers between devices, on_device(): cache_grad = lax.psum(local_grad, 'tp')  137 us
    all_gather x1, waiting for transfers between devices, on_device(): piece_cotan = lax.all_gather(rows_cotan, 'ctx', axis=0, tiled=True)  129 us
    all_gather x1, waiting for transfers between devices, on_device(): gathered = lax.all_gather(latent_cache, 'ctx', axis=0, tiled=True)  102 us
    all_gather x1, blocking collectives, on_device(): lax.all_gather(log_total, 'ctx', axis=0, tiled=True)  48.4 us
    all_gather x1, blocking collectives, on_device(): lax.all_gather(row_delta, 'ctx', axis=0, tiled=True)  46 us
    unnamed x1, blocking collectives  26.8 us
    all_gather x1, waiting for transfers between devices, on_device(): piece_query = lax.all_gather(rows_query, 'ctx', axis=0, tiled=True)  22.5 us
    squeeze x16, local copies, waits for them, and re-layouts, on_device(): lax.scan(stats_step, first_state, (key_blocks, pos_blocks))  18.4 us
  transfers between devices with their start and end apart: 4, of which 4 were waited for; matrix products, arithmetic and copies ran while one was open for 9% of the time, Pallas kernels for 0%

commit v1 on v0

v1 whole, which is shorter than its diff:
```python
import functools

import jax
import jax.numpy as jnp
from jax import lax
from jax.experimental import pallas as pl
from jax.experimental.pallas import tpu as pltpu
from jax.sharding import PartitionSpec as P

ROPE = 64
NOPE = 128
LATENT = 512
WIDTH = LATENT + ROPE
SCALE = (NOPE + ROPE) ** (-0.5)
MESH = pl.DeviceIdType.MESH
MASKED = -1e30
HOPS = (0, 2, -2, 4, -4, 6, -6, 8)


def kernel(
    start_ref, query_ref, cotan_ref, cache_ref,
    dq_ref, dc_ref,
    rows_q, rows_g, keys, probs, gprobs, dkeys, stats, norm,
    dq_part, dq_core, dq_out, dq_in, x_out, x_in, z_out, z_in,
    s_rows, r_q, r_g, s_key, r_zkey, s_fwd, r_xkey, s_stat, r_stat,
    s_core, r_core, s_dq, r_dq, s_x, r_x, s_z, r_z, s_fin, r_fin,
):
    ctx = lax.axis_index("ctx")
    tp = lax.axis_index("tp")
    xl, z = ctx // 16, ctx % 16
    xh, y, k = tp // 8, (tp // 2) % 4, tp % 2
    g = y * 2 + k
    parity = lax.rem(z + xh, 2)

    def dev(xl_=xl, z_=z, xh_=xh, y_=y, k_=k):
        return (xl_ * 16 + z_, (xh_ * 4 + y_) * 2 + k_)

    def remote(src, dst, ss, rs, to):
        return pltpu.make_async_remote_copy(
            src_ref=src, dst_ref=dst, send_sem=ss, recv_sem=rs, device_id=to, device_id_type=MESH
        )

    def ymod(s):
        return lax.rem(y + s, 4)

    def zmod(s):
        return lax.rem(z + s + 32, 16)

    x = xh * 2 + xl

    def xmod(s):
        x_ = lax.rem(x + s, 4)
        return x_ // 2, x_ % 2

    barrier = pltpu.get_barrier_semaphore()
    partners = []
    for s in range(1, 16):
        partners.append(dev(z_=zmod(s)))
    for s in (1, 3):
        hi, lo = xmod(s)
        partners.append(dev(xh_=hi, xl_=lo))
    for h in range(2):
        for s in range(4):
            for c in range(2):
                if h or s or c:
                    partners.append(dev(xh_=xh if h == 0 else 1 - xh, y_=ymod(s), k_=k if c == 0 else 1 - k))
    for p in partners:
        pl.semaphore_signal(barrier, inc=1, device_id=p, device_id_type=MESH)

    rows_q[pl.ds(pl.multiple_of(g * 128, 128), 128), :] = query_ref[...]
    rows_g[pl.ds(pl.multiple_of(g * 128, 128), 128), :] = cotan_ref[...]

    pl.semaphore_wait(barrier, len(partners))

    def rslot(ref, i):
        return ref.at[pl.ds(pl.multiple_of(i * 128, 128), 128), :]

    def kslot(ref, i):
        return ref.at[pl.ds(pl.multiple_of(i * 16, 16), 16), :]

    def block_slot(lo, zz):
        return (lo * 2 + lax.rem(zz, 2)) * 8 + zz // 2

    own_piece = kslot(cache_ref, g)

    def send_key(s):
        return remote(own_piece, kslot(keys, block_slot(xl, z)), s_key.at[s], r_zkey.at[z // 2], dev(z_=zmod(s)))

    order = (8, 7, 9, 6, 10, 5, 11, 4, 12, 3, 13, 2, 14, 1, 15)

    @pl.when(parity == 0)
    def _():
        for s in order:
            send_key(s).start()
        keys[pl.ds(pl.multiple_of(block_slot(xl, z) * 16, 16), 16), :] = cache_ref[
            pl.ds(pl.multiple_of(g * 16, 16), 16), :
        ]

    row_sends = []

    def send_rows(slot, to, i):
        for src, sems in ((rows_q, r_q), (rows_g, r_g)):
            c = remote(rslot(src, slot), rslot(src, slot), s_rows.at[i, 0 if src is rows_q else 1], sems.at[slot], to)
            c.start()
            row_sends.append(c)

    for i, s in enumerate((1, 3, 2)):
        send_rows(g, dev(y_=ymod(s)), i)
    send_rows(g, dev(k_=1 - k), 3)

    def wait_rows(slot):
        for src, sems in ((rows_q, r_q), (rows_g, r_g)):
            remote(rslot(src, slot), rslot(src, slot), s_rows.at[0, 0], sems.at[slot], dev(k_=1 - k)).wait_recv()

    def forward(slot, j, i, s):
        hi, lo = xmod(s)
        return remote(kslot(keys, slot), kslot(keys, slot), s_fwd.at[j, i], r_xkey.at[slot], dev(xh_=hi, xl_=lo))

    for j, hop in enumerate(HOPS):
        zz = zmod(hop - parity)
        slot = block_slot(xl, zz)

        def arrived():
            remote(own_piece, kslot(keys, slot), s_key.at[1], r_zkey.at[zz // 2], dev(z_=zmod(1))).wait_recv()

        if hop == 0:
            pl.when(parity == 1)(arrived)
        else:
            arrived()
        for i, s in enumerate((2, 1, 3)):
            forward(slot, j, i, s).start()

    for i, s in enumerate((1, 3, 2)):
        slot = ymod(s) * 2 + k
        wait_rows(slot)
        send_rows(slot, dev(k_=1 - k), 4 + i)

    for s in (1, 3, 2):
        hi, lo = xmod(s)
        for j in range(8):
            slot = (lo * 2 + hi) * 8 + j
            remote(own_piece, kslot(keys, slot), s_key.at[1], r_xkey.at[slot], dev(z_=zmod(1))).wait_recv()

    start = start_ref[0]
    n = lax.broadcasted_iota(jnp.int32, (512, 1), 0)
    group = n >> 7
    key_pos = (group >> 1) * 2048 + (((n >> 4) & 7) * 2 + (group & 1)) * 128 + g * 16 + (n & 15)
    row_pos = start + ((lax.broadcasted_iota(jnp.int32, (1, 256), 1) & 127) >> 3)
    nt = (((1,), (1,)), ((), ()))
    tn = (((0,), (0,)), ((), ()))

    for s in (0, 1, 3, 2):
        yy = ymod(s)
        wait_rows(yy * 2 + 1 - k)
        rows = pl.ds(pl.multiple_of(yy * 256, 256), 256)
        raw = lax.dot_general(keys[...], rows_q[rows, :], nt, preferred_element_type=jnp.float32) * SCALE
        scores = jnp.where(key_pos <= row_pos, raw, MASKED)
        gp = lax.dot_general(keys[:, :LATENT], rows_g[rows, :], nt, preferred_element_type=jnp.float32)
        top = jnp.max(scores, axis=0, keepdims=True)
        e = jnp.exp(scores - top)
        total = jnp.sum(e, axis=0, keepdims=True)
        dot = jnp.sum(e * gp, axis=0, keepdims=True)
        probs[yy] = e
        gprobs[yy] = gp
        for half in range(2):
            cols = slice(half * 128, half * 128 + 128)
            stats[g, 0, pl.ds(yy * 2 + half, 1), :] = top[:, cols]
            stats[g, 1, pl.ds(yy * 2 + half, 1), :] = total[:, cols]
            stats[g, 2, pl.ds(yy * 2 + half, 1), :] = dot[:, cols]

    stat_sends = []
    for s in range(4):
        for c in range(2):
            if s or c:
                copy = remote(
                    stats.at[g], stats.at[g], s_stat.at[s * 2 + c], r_stat.at[g],
                    dev(y_=ymod(s), k_=k if c == 0 else 1 - k),
                )
                copy.start()
                stat_sends.append(copy)
    for s in range(4):
        for c in range(2):
            if s or c:
                other = ymod(s) * 2 + (k if c == 0 else 1 - k)
                remote(stats.at[g], stats.at[other], s_stat.at[1], r_stat.at[other], dev(k_=1 - k)).wait_recv()

    tops = [stats[i, 0] for i in range(8)]
    top = functools.reduce(jnp.maximum, tops)
    weights = [jnp.exp(t - top) for t in tops]
    total = sum(w * stats[i, 1] for i, w in enumerate(weights))
    delta = sum(w * stats[i, 2] for i, w in enumerate(weights)) / total
    own_top = stats[g, 0]
    factor = jnp.exp(own_top - top) / total
    norm[0] = factor
    norm[1] = delta

    core_sends = []
    for at, s in enumerate((1, 3, 2, 0)):
        yy = ymod(s)
        rows = pl.ds(pl.multiple_of(yy * 256, 256), 256)
        f = jnp.concatenate([norm[0, pl.ds(yy * 2 + h, 1), :] for h in range(2)], axis=1)
        d = jnp.concatenate([norm[1, pl.ds(yy * 2 + h, 1), :] for h in range(2)], axis=1)
        p = probs[yy] * f
        gs = (p * (gprobs[yy] - d)).astype(jnp.bfloat16)
        low = p.astype(jnp.bfloat16)
        key_term = SCALE * jnp.dot(gs, rows_q[rows, :], preferred_element_type=jnp.float32)
        value_term = jnp.dot(low, rows_g[rows, :], preferred_element_type=jnp.float32)
        if at == 0:
            dkeys[...] = key_term
        else:
            dkeys[...] += key_term
        dkeys[:, :LATENT] += value_term
        part = lax.dot_general(gs, keys[...], tn, preferred_element_type=jnp.float32) * SCALE
        dq_part[at] = part.reshape(2, 128, WIDTH)
        copy = remote(dq_part.at[at, 1 - k], dq_core.at[at], s_core.at[at], r_core.at[at], dev(k_=1 - k))
        copy.start()
        core_sends.append(copy)

    x_sends = []
    for i, s in enumerate((2, 1, 3)):
        hi, lo = xmod(s)
        x_out[i] = dkeys[pl.ds(pl.multiple_of((lo * 2 + hi) * 128, 128), 128), :].astype(jnp.bfloat16)
        copy = remote(x_out.at[i], x_in.at[i], s_x.at[i], r_x.at[i], dev(xh_=hi, xl_=lo))
        copy.start()
        x_sends.append(copy)

    dq_sends = []
    for at, s in enumerate((1, 3, 2)):
        core_sends[at].wait_recv()
        dq_out[at] = dq_part[at, k] + dq_core[at]
        copy = remote(dq_out.at[at], dq_in.at[at], s_dq.at[at], r_dq.at[at], dev(y_=ymod(s)))
        copy.start()
        dq_sends.append(copy)
    core_sends[3].wait_recv()

    for copy in x_sends:
        copy.wait_recv()
    mine = dkeys[pl.ds(pl.multiple_of((xl * 2 + xh) * 128, 128), 128), :]
    for i in range(3):
        mine = mine + x_in[i].astype(jnp.float32)
    dkeys[pl.ds(0, 128), :] = mine
    z_out[...] = mine.astype(jnp.bfloat16)

    def z_send(j, hop):
        zz = zmod(hop - parity)
        return remote(kslot(z_out, zz // 2), z_in.at[z], s_z.at[j], r_z.at[z], dev(z_=zz))

    for j in reversed(range(8)):
        if HOPS[j] == 0:
            pl.when(parity == 1)(lambda: z_send(0, 0).start())
        else:
            z_send(j, HOPS[j]).start()

    dq = dq_part[3, k] + dq_core[3]
    for copy in dq_sends:
        copy.wait_recv()
    for at in range(3):
        dq = dq + dq_in[at]
    dq_ref[...] = dq.astype(jnp.bfloat16)

    fin = []
    for h in range(2):
        for s in range(4):
            for c in range(2):
                if h or s or c:
                    fin.append(dev(xh_=xh if h == 0 else 1 - xh, y_=ymod(s), k_=k if c == 0 else 1 - k))

    def fin_send(i):
        return remote(kslot(dc_ref, g), kslot(dc_ref, g), s_fin.at[i], r_fin.at[g], fin[i])

    @pl.when(parity == 0)
    def _():
        acc = dkeys[pl.ds(pl.multiple_of((z // 2) * 16, 16), 16), :]
        for s in range(1, 16):
            zz = zmod(s)
            remote(kslot(z_out, 0), z_in.at[zz], s_z.at[0], r_z.at[zz], dev(z_=zz)).wait_recv()
            acc = acc + z_in[zz].astype(jnp.float32)
        dc_ref[pl.ds(pl.multiple_of(g * 16, 16), 16), :] = acc
        for i in range(15):
            fin_send(i).start()
        for i in range(15):
            fin_send(i).wait_send()
        for s in order:
            send_key(s).wait_send()

    for s in range(4):
        for c in range(2):
            other = ymod(s) * 2 + (k if c == 0 else 1 - k)

            def wait_fin():
                remote(kslot(dc_ref, other), kslot(dc_ref, other), s_fin.at[0], r_fin.at[other], dev(k_=1 - k)).wait_recv()

            if s or c:
                wait_fin()
            else:
                pl.when(parity == 1)(wait_fin)

    for copy in row_sends + stat_sends + core_sends + x_sends + dq_sends:
        copy.wait_send()
    for j, hop in enumerate(HOPS):
        zz = zmod(hop - parity)
        slot = block_slot(xl, zz)
        for i, s in enumerate((2, 1, 3)):
            forward(slot, j, i, s).wait_send()
        if hop == 0:
            pl.when(parity == 1)(lambda: z_send(0, 0).wait_send())
        else:
            z_send(j, hop).wait_send()


def on_device(queries, grad_out, latent_cache, slab_starts):
    f32, bf16 = jnp.float32, jnp.bfloat16
    dma = pltpu.SemaphoreType.DMA
    vmem = pl.BlockSpec(memory_space=pltpu.VMEM)
    query_grad, cache_grad = pl.pallas_call(
        kernel,
        out_shape=(
            jax.ShapeDtypeStruct((128, WIDTH), bf16),
            jax.ShapeDtypeStruct((128, WIDTH), f32),
        ),
        in_specs=[pl.BlockSpec(memory_space=pltpu.SMEM), vmem, vmem, vmem],
        out_specs=[vmem, vmem],
        scratch_shapes=[
            pltpu.VMEM((1024, WIDTH), bf16),
            pltpu.VMEM((1024, LATENT), bf16),
            pltpu.VMEM((512, WIDTH), bf16),
            pltpu.VMEM((4, 512, 256), f32),
            pltpu.VMEM((4, 512, 256), f32),
            pltpu.VMEM((512, WIDTH), f32),
            pltpu.VMEM((8, 3, 8, 128), f32),
            pltpu.VMEM((2, 8, 128), f32),
            pltpu.VMEM((4, 2, 128, WIDTH), f32),
            pltpu.VMEM((4, 128, WIDTH), f32),
            pltpu.VMEM((3, 128, WIDTH), f32),
            pltpu.VMEM((3, 128, WIDTH), f32),
            pltpu.VMEM((3, 128, WIDTH), bf16),
            pltpu.VMEM((3, 128, WIDTH), bf16),
            pltpu.VMEM((128, WIDTH), bf16),
            pltpu.VMEM((16, 16, WIDTH), bf16),
            dma((7, 2)), dma((8,)), dma((8,)),
            dma((16,)), dma((8,)), dma((8, 3)), dma((32,)),
            dma((8,)), dma((8,)),
            dma((4,)), dma((4,)), dma((3,)), dma((3,)),
            dma((3,)), dma((3,)), dma((8,)), dma((16,)),
            dma((15,)), dma((8,)),
        ],
        compiler_params=pltpu.CompilerParams(
            collective_id=0, has_side_effects=True, vmem_limit_bytes=40 << 20
        ),
        cost_estimate=pl.CostEstimate(flops=2886000000, bytes_accessed=900000, transcendentals=530000),
        name="latent_attention_backward",
    )(
        slab_starts,
        queries.reshape(128, WIDTH),
        grad_out.reshape(128, LATENT),
        latent_cache,
    )
    return query_grad.reshape(queries.shape), cache_grad


def solution(mesh):
    placed = (P("ctx", "tp", None), P("ctx", "tp", None), P("ctx", None), P("ctx"))
    return jax.shard_map(
        on_device,
        mesh=mesh,
        in_specs=placed,
        out_specs=(P("ctx", "tp", None), P("ctx", None)),
        check_vma=False,
    )
```

time: 598 us -> 79.9 us (0.13)
  the two profiles are of different devices: /device:TPU:1 before, /device:TPU:33 now
where the time goes in v1:
time: 79.9 us; the launch traced here: 79.8 us
  Pallas kernels  75.8 us (95%)
  local copies, waits for them, and re-layouts  2.64 us (3%)
  between operations  1.35 us (2%)
    pallas_call x1, Pallas kernels, on_device(): pl.pallas_call(kernel, out_shape=(jax.ShapeDtypeStruct((128, WIDTH), bf16...  75.8 us
    unnamed x7, local copies, waits for them, and re-layouts  2.64 us

profile of v1, /device:TPU:33, one launch (start us, length us, event | category | flops | bytes accessed | tf_op | source)
XLA Modules:
  0.0 79.8 jit_solution(5586070967748286675)
XLA Ops:
  0.6 0.0 copy-start
  1.3 0.0 copy-start.1
  1.3 1.1 %copy.6.cache_ref = bf16[128,576]{1,0:T(8,128)(2,1)S(1)} copy(bf16[128,576]{0,1:T(8,128)(2,1)} %param.6) | data formatting | bytes 294912 | tf_op args[2]
  2.4 0.0 copy-done
  2.4 0.0 copy-done.1
  2.4 75.8 %latent_attention_backward.1 = (bf16[128,576]{1,0:T(8,128)(2,1)S(1)}, f32[128,576]{1,0:T(8,128)S(1)}) custom-call(s32[1]{0:T(128)S(6)} %copy.9.start_ref, bf16[128,576]{1,0:T(8,128)(2,1)S(1)} %bitcast.4, bf16[128,512]{1,0:T(8,128)(2,1)S(1)} %bitcast.5, bf16[128,576]{1,0:T(8,128)(2,1)S(1)} %copy.6.cache_ref), custom_call_target="tpu_custom_call" | custom-call | flops 2886000128 | bytes 900000 | tf_op jit(solution)/shard_map/latent_attention_backward/pallas_call | solution.py:315
  78.2 0.9 %copy.7 = f32[128,576]{0,1:T(8,128)} copy(f32[128,576]{1,0:T(8,128)S(1)} %get-tuple-element.7) | data formatting | bytes 589824
  79.1 0.7 copy.10
Async XLA Ops:
  0.6 1.8 %copy-start = (bf16[16,8,576]{2,1,0:T(8,128)(2,1)S(1)}, bf16[16,8,576]{2,1,0:T(8,128)(2,1)}, u32[]{:S(2)}) copy-start(bf16[16,8,576]{2,1,0:T(8,128)(2,1)} %param.4) | copy-start | bytes 442372
  1.3 1.1 %copy-start.1 = (bf16[16,8,512]{2,1,0:T(8,128)(2,1)S(1)}, bf16[16,8,512]{2,1,0:T(8,128)(2,1)}, u32[]{:S(2)}) copy-start(bf16[16,8,512]{2,1,0:T(8,128)(2,1)} %param.5) | copy-start | bytes 393220

commit v2 on v1

v2 whole, which is shorter than its diff:
```python
import functools

import jax
import jax.numpy as jnp
from jax import lax
from jax.experimental import pallas as pl
from jax.experimental.pallas import tpu as pltpu
from jax.sharding import PartitionSpec as P

ROPE = 64
NOPE = 128
LATENT = 512
WIDTH = LATENT + ROPE
SCALE = (NOPE + ROPE) ** (-0.5)
MESH = pl.DeviceIdType.MESH
MASKED = -1e30
HOPS = (6, 8, 10, 12, -2, 0, 2, 4)
OWN = 5
ARRIVE = (5, 6, 4, 7, 3, 0, 2, 1)
FAR = (8, 7, 9, 6, 10, 5, 11, 4, 12, 3, 13, 2, 14, 1, 15)
NEAR = FAR[::-1]


def kernel(
    start_ref, query_ref, cotan_ref, cache_ref,
    dq_ref, dc_ref,
    rows_q, rows_g, keys, probs, gprobs, gscores, plow, dkeys, stats,
    dq_part, dq_core, dq_out, dq_in, x_out, x_in, z_out, z_in, done,
    s_rows, r_q, r_g, s_key, r_zkey, s_fwd, r_xkey, s_stat, r_stat,
    s_core, r_core, s_dq, r_dq, s_x, r_x, s_z, r_z, s_fin, r_fin,
):
    ctx = lax.axis_index("ctx")
    tp = lax.axis_index("tp")
    xl, z = ctx // 16, ctx % 16
    xh, y, k = tp // 8, (tp // 2) % 4, tp % 2
    x = xh * 2 + xl
    g = y * 2 + k
    parity = lax.rem(z + xh, 2)

    def dev(xl_=xl, z_=z, xh_=xh, y_=y, k_=k):
        return (xl_ * 16 + z_, (xh_ * 4 + y_) * 2 + k_)

    def remote(src, dst, ss, rs, to):
        return pltpu.make_async_remote_copy(
            src_ref=src, dst_ref=dst, send_sem=ss, recv_sem=rs, device_id=to, device_id_type=MESH
        )

    def ymod(s):
        return lax.rem(y + s, 4)

    def zmod(s):
        return lax.rem(z + s + 32, 16)

    def xdev(s):
        x_ = lax.rem(x + s, 4)
        return dev(xh_=x_ // 2, xl_=x_ % 2)

    core = dev(k_=1 - k)

    barrier = pltpu.get_barrier_semaphore()
    partners = [dev(z_=zmod(s)) for s in FAR]
    partners += [xdev(1), xdev(3)]
    for h in range(2):
        for s in range(4):
            for c in range(2):
                if h or s or c:
                    partners.append(dev(xh_=xh if h == 0 else 1 - xh, y_=ymod(s), k_=k if c == 0 else 1 - k))
    for p in partners:
        pl.semaphore_signal(barrier, inc=1, device_id=p, device_id_type=MESH)

    def rslot(ref, i):
        return ref.at[pl.ds(pl.multiple_of(i * 128, 128), 128), :]

    def kslot(ref, i):
        return ref.at[pl.ds(pl.multiple_of(i * 16, 16), 16), :]

    own_rows = pl.ds(pl.multiple_of(g * 128, 128), 128)
    rows_q[own_rows, :] = query_ref[...]
    rows_g[own_rows, :] = cotan_ref[...]

    pl.semaphore_wait(barrier, len(partners))

    own_piece = kslot(cache_ref, g)

    def key_slot(r, j):
        return (j // 4) * 16 + ((r if j >= 4 else r + 3) % 4) * 4 + j % 4

    def send_key(s):
        j = next(j for j in range(8) if (HOPS[j] - s % 2 + s) % 16 == 0)
        return remote(own_piece, kslot(keys, key_slot(0, j)), s_key.at[s], r_zkey.at[j], dev(z_=zmod(s)))

    @pl.when(parity == 0)
    def _():
        for s in NEAR:
            send_key(s).start()
        keys[key_slot(0, OWN) * 16 : key_slot(0, OWN) * 16 + 16, :] = cache_ref[
            pl.ds(pl.multiple_of(g * 16, 16), 16), :
        ]

    row_sends = []

    def send_rows(n, slot, to):
        src, sems = ((rows_q, r_q), (rows_g, r_g))[n]
        c = remote(rslot(src, slot), rslot(src, slot), s_rows.at[len(row_sends)], sems.at[slot], to)
        c.start()
        row_sends.append(c)

    def wait_rows(n, slot):
        src, sems = ((rows_q, r_q), (rows_g, r_g))[n]
        remote(rslot(src, slot), rslot(src, slot), s_rows.at[0], sems.at[slot], core).wait_recv()

    right, left = dev(y_=ymod(1)), dev(y_=ymod(3))
    send_rows(0, g, right)
    send_rows(1, g, left)
    send_rows(1, g, right)
    send_rows(0, g, left)
    send_rows(0, g, core)
    send_rows(1, g, core)

    def forward(j, s):
        return remote(
            kslot(keys, key_slot(0, j)), kslot(keys, key_slot(4 - s, j)),
            s_fwd.at[j, s - 1], r_xkey.at[4 - s, j], xdev(s),
        )

    def pass_on(j):
        def arrived():
            remote(own_piece, kslot(keys, key_slot(0, j)), s_key.at[1], r_zkey.at[j], core).wait_recv()

        if j == OWN:
            pl.when(parity == 1)(arrived)
        else:
            arrived()
        for s in (2, 1, 3):
            forward(j, s).start()

    def pass_rows(s, n, ring):
        slot = ymod(s) * 2 + k
        wait_rows(n, slot)
        if ring is not None:
            send_rows(n, slot, ring)
        send_rows(n, slot, core)

    for j in ARRIVE[:4]:
        pass_on(j)
    pass_rows(3, 0, right)
    pass_rows(1, 1, left)
    for j in ARRIVE[4:6]:
        pass_on(j)
    pass_rows(3, 1, None)
    pass_rows(1, 0, None)
    for j in ARRIVE[6:]:
        pass_on(j)
    pass_rows(2, 0, None)
    pass_rows(2, 1, None)
    for n in range(2):
        wait_rows(n, g + 1 - 2 * k)

    nt = (((1,), (1,)), ((), ()))
    tn = (((0,), (0,)), ((), ()))
    row_pos = start_ref[0] + ((lax.broadcasted_iota(jnp.int32, (1, 256), 1) & 127) >> 3)

    def products(first, size, b):
        span = slice(first, first + size)
        n = first + lax.broadcasted_iota(jnp.int32, (size, 1), 0)
        half = n >> 8
        chip = (x + (n >> 6) + 1 - half) & 3
        hop = ((n >> 4) & 3) * 2 + 6 - 8 * half
        z_key = (z + hop - ((z + (chip >> 1)) & 1)) & 15
        key_pos = ((chip & 1) * 16 + z_key) * 128 + g * 16 + (n & 15)
        rows = pl.ds(pl.multiple_of(b * 256, 256), 256)
        raw = lax.dot_general(keys[span, :], rows_q[rows, :], nt, preferred_element_type=jnp.float32) * SCALE
        gp = lax.dot_general(keys[span, :LATENT], rows_g[rows, :], nt, preferred_element_type=jnp.float32)
        return jnp.where(key_pos <= row_pos, raw, MASKED), gp

    def keep_products(first, size, b):
        span = slice(first, first + size)
        scores, gp = products(first, size, b)
        probs[b, span, :] = scores
        gprobs[b, span, :] = gp

    for s in (0, 1, 3, 2):
        if s:
            for n in range(2):
                wait_rows(n, ymod(s) * 2 + 1 - k)
        keep_products(192, 128, ymod(s))

    def wait_keys(places):
        for j in places:
            for r in (1, 3, 2):
                slot = kslot(keys, key_slot(r, j))
                remote(own_piece, slot, s_key.at[1], r_xkey.at[r, j], core).wait_recv()

    wait_keys(ARRIVE[:4])
    for b in range(4):
        keep_products(320, 192, b)
    wait_keys(ARRIVE[4:])

    stat_sends = []
    for b in range(4):
        low, low_gp = products(0, 192, b)
        rest = probs[b, 192:, :]
        top = jnp.max(low, axis=0, keepdims=True)
        top = jnp.maximum(top, jnp.max(rest, axis=0, keepdims=True))
        total = dot = 0.0
        for span, part, gp in ((slice(0, 192), low, low_gp), (slice(192, 512), rest, gprobs[b, 192:, :])):
            e = jnp.exp(part - top)
            total = total + jnp.sum(e, axis=0, keepdims=True)
            dot = dot + jnp.sum(e * gp, axis=0, keepdims=True)
            probs[b, span, :] = e
        gprobs[b, :192, :] = low_gp
        for i, v in enumerate((top, total, dot)):
            for h in range(2):
                stats[g, b // 2, pl.ds(i * 4 + (b % 2) * 2 + h, 1), :] = v[:, h * 128 : h * 128 + 128]
        if b % 2:
            half = stats.at[g, b // 2]
            for s in (2, 1, 3, 0):
                for c in range(2):
                    if s or c:
                        copy = remote(
                            half, half, s_stat.at[b // 2, s * 2 + c], r_stat.at[b // 2, g],
                            dev(y_=ymod(s), k_=k if c == 0 else 1 - k),
                        )
                        copy.start()
                        stat_sends.append(copy)

    def normalize(half):
        for s in range(4):
            for c in range(2):
                if s or c:
                    other = ymod(s) * 2 + (k if c == 0 else 1 - k)
                    at = stats.at[other, half]
                    remote(at, at, s_stat.at[0, 0], r_stat.at[half, other], core).wait_recv()
        tops = [stats[i, half, :4, :] for i in range(8)]
        top = functools.reduce(jnp.maximum, tops)
        weights = [jnp.exp(t - top) for t in tops]
        total = sum(w * stats[i, half, 4:8, :] for i, w in enumerate(weights))
        delta = sum(w * stats[i, half, 8:12, :] for i, w in enumerate(weights)) / total
        factor = jnp.exp(stats[g, half, :4, :] - top) / total
        flat = lambda v: [jnp.concatenate([v[2 * i : 2 * i + 1], v[2 * i + 1 : 2 * i + 2]], axis=1) for i in range(2)]
        return flat(factor), flat(delta)

    def second(span, half, factor, delta):
        for i in range(2):
            b = half * 2 + i
            cols = slice(b * 256, b * 256 + 256)
            p = probs[b, span, :] * factor[i]
            gscores[span, cols] = (p * (gprobs[b, span, :] - delta[i])).astype(jnp.bfloat16)
            plow[span, cols] = p.astype(jnp.bfloat16)
        rows = slice(half * 512, half * 512 + 512)
        key_term = SCALE * jnp.dot(gscores[span, rows], rows_q[rows, :], preferred_element_type=jnp.float32)
        value_term = jnp.dot(plow[span, rows], rows_g[rows, :], preferred_element_type=jnp.float32)
        if half == 0:
            dkeys[span, :] = key_term
        else:
            dkeys[span, :] += key_term
        dkeys[span, :LATENT] += value_term

    factor, delta = normalize(0)
    second(slice(0, 512), 0, factor, delta)
    factor, delta = normalize(1)
    x_sends = []
    for half in range(2):
        second(slice(half * 256, half * 256 + 256), 1, factor, delta)
        for s in (2, 1, 3):
            at = key_slot(s, half * 4) * 16
            x_out[s - 1, half] = dkeys[at : at + 64, :].astype(jnp.bfloat16)
            copy = remote(
                x_out.at[s - 1, half], x_in.at[s - 1, half], s_x.at[s - 1, half], r_x.at[s - 1, half], xdev(s)
            )
            copy.start()
            x_sends.append(copy)

    core_sends = []
    hops_y = (2, 1, 3, 0)

    def query_part(at):
        cols = pl.ds(pl.multiple_of(ymod(hops_y[at]) * 256, 256), 256)
        part = lax.dot_general(gscores[:, cols], keys[...], tn, preferred_element_type=jnp.float32) * SCALE
        dq_part[at] = part.reshape(2, 128, WIDTH)
        copy = remote(dq_part.at[at, 1 - k], dq_core.at[at], s_core.at[at], r_core.at[at], core)
        copy.start()
        core_sends.append(copy)

    def z_send(j):
        return remote(kslot(z_out, j), z_in.at[z], s_z.at[j], r_z.at[z], dev(z_=zmod(HOPS[j] - parity)))

    def sum_x(half):
        at = key_slot(0, half * 4) * 16
        mine = dkeys[at : at + 64, :]
        for i, s in enumerate((2, 1, 3)):
            x_sends[half * 3 + i].wait_recv()
            mine = mine + x_in[s - 1, half].astype(jnp.float32)
        dkeys[at : at + 64, :] = mine
        z_out[half * 64 : half * 64 + 64, :] = mine.astype(jnp.bfloat16)
        for j in ((1, 2, 0, 3), (7, 4, 6, 5))[half]:
            if j == OWN:
                pl.when(parity == 1)(lambda: z_send(OWN).start())
            else:
                z_send(j).start()

    for at in range(4):
        query_part(at)
    dq_sends = []
    for at, s in enumerate(hops_y[:3]):
        core_sends[at].wait_recv()
        dq_out[at] = (dq_part[at, k] + dq_core[at]).astype(jnp.bfloat16)
        copy = remote(dq_out.at[at], dq_in.at[at], s_dq.at[at], r_dq.at[at], dev(y_=ymod(s)))
        copy.start()
        dq_sends.append(copy)
    sum_x(0)
    sum_x(1)

    fin = [dev(xh_=1 - xh, y_=ymod(s)) for s in (2, 1, 3, 0)] + [dev(y_=ymod(s)) for s in (2, 1, 3)]

    def fin_send(slot, i, to):
        return remote(kslot(done, slot), kslot(done, slot), s_fin.at[i], r_fin.at[slot], to)

    def wait_fin(slot):
        fin_send(slot, 0, core).wait_recv()

    @pl.when(parity == 0)
    def _():
        at = key_slot(0, OWN) * 16
        acc = dkeys[at : at + 16, :]
        for s in NEAR:
            zz = zmod(s)
            remote(kslot(z_out, 0), z_in.at[zz], s_z.at[0], r_z.at[zz], core).wait_recv()
            acc = acc + z_in[zz].astype(jnp.float32)
        done[pl.ds(pl.multiple_of(g * 16, 16), 16), :] = acc.astype(jnp.bfloat16)
        for i, to in enumerate(fin):
            fin_send(g, i, to).start()

    core_sends[3].wait_recv()
    dq = dq_part[3, k] + dq_core[3]
    for copy in dq_sends:
        copy.wait_recv()
    for at in range(3):
        dq = dq + dq_in[at].astype(jnp.float32)
    dq_ref[...] = dq.astype(jnp.bfloat16)

    for i, s in enumerate((0, 1, 3, 2)):
        slot = ymod(s) * 2 + k
        if s == 0:
            pl.when(parity == 1)(lambda: wait_fin(slot))
        else:
            wait_fin(slot)
        fin_send(slot, 7 + i, core).start()
    for s in (0, 1, 3, 2):
        wait_fin(ymod(s) * 2 + 1 - k)
    dc_ref[...] = done[...].astype(jnp.float32)

    @pl.when(parity == 0)
    def _():
        for s in FAR:
            send_key(s).wait_send()
        for i, to in enumerate(fin):
            fin_send(g, i, to).wait_send()

    for i in range(4):
        fin_send(g, 7 + i, core).wait_send()
    for copy in row_sends + stat_sends + core_sends + x_sends + dq_sends:
        copy.wait_send()
    for j in range(8):
        for s in (2, 1, 3):
            forward(j, s).wait_send()
        if j == OWN:
            pl.when(parity == 1)(lambda: z_send(OWN).wait_send())
        else:
            z_send(j).wait_send()


def on_device(queries, grad_out, latent_cache, slab_starts):
    f32, bf16 = jnp.float32, jnp.bfloat16
    dma = pltpu.SemaphoreType.DMA
    vmem = pl.BlockSpec(memory_space=pltpu.VMEM)
    query_grad, cache_grad = pl.pallas_call(
        kernel,
        out_shape=(
            jax.ShapeDtypeStruct((128, WIDTH), bf16),
            jax.ShapeDtypeStruct((128, WIDTH), f32),
        ),
        in_specs=[pl.BlockSpec(memory_space=pltpu.SMEM), vmem, vmem, vmem],
        out_specs=[vmem, vmem],
        scratch_shapes=[
            pltpu.VMEM((1024, WIDTH), bf16),
            pltpu.VMEM((1024, LATENT), bf16),
            pltpu.VMEM((512, WIDTH), bf16),
            pltpu.VMEM((4, 512, 256), f32),
            pltpu.VMEM((4, 512, 256), f32),
            pltpu.VMEM((512, 1024), bf16),
            pltpu.VMEM((512, 1024), bf16),
            pltpu.VMEM((512, WIDTH), f32),
            pltpu.VMEM((8, 2, 16, 128), f32),
            pltpu.VMEM((4, 2, 128, WIDTH), f32),
            pltpu.VMEM((4, 128, WIDTH), f32),
            pltpu.VMEM((3, 128, WIDTH), bf16),
            pltpu.VMEM((3, 128, WIDTH), bf16),
            pltpu.VMEM((3, 2, 64, WIDTH), bf16),
            pltpu.VMEM((3, 2, 64, WIDTH), bf16),
            pltpu.VMEM((128, WIDTH), bf16),
            pltpu.VMEM((16, 16, WIDTH), bf16),
            pltpu.VMEM((128, WIDTH), bf16),
            dma((14,)), dma((8,)), dma((8,)),
            dma((16,)), dma((8,)), dma((8, 3)), dma((4, 8)),
            dma((2, 8)), dma((2, 8)),
            dma((4,)), dma((4,)), dma((3,)), dma((3,)),
            dma((3, 2)), dma((3, 2)), dma((8,)), dma((16,)),
            dma((11,)), dma((8,)),
        ],
        compiler_params=pltpu.CompilerParams(
            collective_id=0, has_side_effects=True, vmem_limit_bytes=40 << 20
        ),
        cost_estimate=pl.CostEstimate(flops=2886000000, bytes_accessed=900000, transcendentals=530000),
        name="latent_attention_backward",
    )(
        slab_starts,
        queries.reshape(128, WIDTH),
        grad_out.reshape(128, LATENT),
        latent_cache,
    )
    return query_grad.reshape(queries.shape), cache_grad


def solution(mesh):
    placed = (P("ctx", "tp", None), P("ctx", "tp", None), P("ctx", None), P("ctx"))
    return jax.shard_map(
        on_device,
        mesh=mesh,
        in_specs=placed,
        out_specs=(P("ctx", "tp", None), P("ctx", None)),
        check_vma=False,
    )
```

time: 79.9 us -> 70.2 us (0.88)
  the two profiles are of different devices: /device:TPU:33 before, /device:TPU:1 now
where the time goes in v2:
time: 70.2 us; the launch traced here: 70 us
  Pallas kernels  66.1 us (94%)
  local copies, waits for them, and re-layouts  2.64 us (4%)
  between operations  1.35 us (2%)
    pallas_call x1, Pallas kernels, on_device(): pl.pallas_call(kernel, out_shape=(jax.ShapeDtypeStruct((128, WIDTH), bf16...  66.1 us
    unnamed x7, local copies, waits for them, and re-layouts  2.64 us

profile of v2, /device:TPU:1, one launch (start us, length us, event | category | flops | bytes accessed | tf_op | source)
XLA Modules:
  0.0 70.0 jit_solution(1224613458986183505)
XLA Ops:
  0.6 0.0 copy-start
  1.3 0.0 copy-start.1
  1.3 1.1 %copy.6.cache_ref = bf16[128,576]{1,0:T(8,128)(2,1)S(1)} copy(bf16[128,576]{0,1:T(8,128)(2,1)} %param.6) | data formatting | bytes 294912 | tf_op args[2]
  2.4 0.0 copy-done
  2.4 0.0 copy-done.1
  2.4 66.1 %latent_attention_backward.1 = (bf16[128,576]{1,0:T(8,128)(2,1)S(1)}, f32[128,576]{1,0:T(8,128)S(1)}) custom-call(s32[1]{0:T(128)S(6)} %copy.9.start_ref, bf16[128,576]{1,0:T(8,128)(2,1)S(1)} %bitcast.4, bf16[128,512]{1,0:T(8,128)(2,1)S(1)} %bitcast.5, bf16[128,576]{1,0:T(8,128)(2,1)S(1)} %copy.6.cache_ref), custom_call_target="tpu_custom_call" | custom-call | flops 2886000128 | bytes 900000 | tf_op jit(solution)/shard_map/latent_attention_backward/pallas_call | solution.py:377
  68.5 0.9 %copy.7 = f32[128,576]{0,1:T(8,128)} copy(f32[128,576]{1,0:T(8,128)S(1)} %get-tuple-element.7) | data formatting | bytes 589824
  69.4 0.7 copy.10
Async XLA Ops:
  0.6 1.8 %copy-start = (bf16[16,8,576]{2,1,0:T(8,128)(2,1)S(1)}, bf16[16,8,576]{2,1,0:T(8,128)(2,1)}, u32[]{:S(2)}) copy-start(bf16[16,8,576]{2,1,0:T(8,128)(2,1)} %param.4) | copy-start | bytes 442372
  1.3 1.1 %copy-start.1 = (bf16[16,8,512]{2,1,0:T(8,128)(2,1)S(1)}, bf16[16,8,512]{2,1,0:T(8,128)(2,1)}, u32[]{:S(2)}) copy-start(bf16[16,8,512]{2,1,0:T(8,128)(2,1)} %param.5) | copy-start | bytes 393220

commit v3 on v2

--- a/solution.py
+++ b/solution.py
@@ -17,6 +17,7 @@
 HOPS = (6, 8, 10, 12, -2, 0, 2, 4)
 OWN = 5
 ARRIVE = (5, 6, 4, 7, 3, 0, 2, 1)
+LEAVE = (1, 2, 0, 3, 7, 4, 6, 5)
 FAR = (8, 7, 9, 6, 10, 5, 11, 4, 12, 3, 13, 2, 14, 1, 15)
 NEAR = FAR[::-1]
 
@@ -63,7 +64,7 @@
     for h in range(2):
         for s in range(4):
             for c in range(2):
-                if h or s or c:
+                if (c == 0 and (h or s)) or (c and not h):
                     partners.append(dev(xh_=xh if h == 0 else 1 - xh, y_=ymod(s), k_=k if c == 0 else 1 - k))
     for p in partners:
         pl.semaphore_signal(barrier, inc=1, device_id=p, device_id_type=MESH)
@@ -191,24 +192,31 @@
                 slot = kslot(keys, key_slot(r, j))
                 remote(own_piece, slot, s_key.at[1], r_xkey.at[r, j], core).wait_recv()
 
+    def reduce_tile(span, b, scores, gp):
+        top = jnp.max(scores, axis=0, keepdims=True)
+        e = jnp.exp(scores - top)
+        probs[b, span, :] = e
+        return top, jnp.sum(e, axis=0, keepdims=True), jnp.sum(e * gp, axis=0, keepdims=True)
+
     wait_keys(ARRIVE[:4])
+    rest = []
     for b in range(4):
         keep_products(320, 192, b)
+        rest.append(reduce_tile(slice(192, 512), b, probs[b, 192:, :], gprobs[b, 192:, :]))
     wait_keys(ARRIVE[4:])
 
     stat_sends = []
+    scales = []
     for b in range(4):
-        low, low_gp = products(0, 192, b)
-        rest = probs[b, 192:, :]
-        top = jnp.max(low, axis=0, keepdims=True)
-        top = jnp.maximum(top, jnp.max(rest, axis=0, keepdims=True))
-        total = dot = 0.0
-        for span, part, gp in ((slice(0, 192), low, low_gp), (slice(192, 512), rest, gprobs[b, 192:, :])):
-            e = jnp.exp(part - top)
-            total = total + jnp.sum(e, axis=0, keepdims=True)
-            dot = dot + jnp.sum(e * gp, axis=0, keepdims=True)
-            probs[b, span, :] = e
-        gprobs[b, :192, :] = low_gp
+        scores, gp = products(0, 192, b)
+        gprobs[b, :192, :] = gp
+        top0, total0, dot0 = reduce_tile(slice(0, 192), b, scores, gp)
+        top1, total1, dot1 = rest[b]
+        top = jnp.maximum(top0, top1)
+        w0, w1 = jnp.exp(top0 - top), jnp.exp(top1 - top)
+        scales.append((w0, w1))
+        total = total0 * w0 + total1 * w1
+        dot = dot0 * w0 + dot1 * w1
         for i, v in enumerate((top, total, dot)):
             for h in range(2):
                 stats[g, b // 2, pl.ds(i * 4 + (b % 2) * 2 + h, 1), :] = v[:, h * 128 : h * 128 + 128]
@@ -244,9 +252,11 @@
         for i in range(2):
             b = half * 2 + i
             cols = slice(b * 256, b * 256 + 256)
-            p = probs[b, span, :] * factor[i]
-            gscores[span, cols] = (p * (gprobs[b, span, :] - delta[i])).astype(jnp.bfloat16)
-            plow[span, cols] = p.astype(jnp.bfloat16)
+            for part, w in ((slice(span.start, min(span.stop, 192)), 0), (slice(max(span.start, 192), span.stop), 1)):
+                if part.start < part.stop:
+                    p = probs[b, part, :] * (factor[i] * scales[b][w])
+                    gscores[part, cols] = (p * (gprobs[b, part, :] - delta[i])).astype(jnp.bfloat16)
+                    plow[part, cols] = p.astype(jnp.bfloat16)
         rows = slice(half * 512, half * 512 + 512)
         key_term = SCALE * jnp.dot(gscores[span, rows], rows_q[rows, :], preferred_element_type=jnp.float32)
         value_term = jnp.dot(plow[span, rows], rows_g[rows, :], preferred_element_type=jnp.float32)
@@ -259,17 +269,20 @@
     factor, delta = normalize(0)
     second(slice(0, 512), 0, factor, delta)
     factor, delta = normalize(1)
-    x_sends = []
+
+    def x_send(s, j):
+        return remote(
+            kslot(x_out.at[s - 1], j), kslot(x_in.at[s - 1], j), s_x.at[s - 1, j], r_x.at[s - 1, j], xdev(s)
+        )
+
     for half in range(2):
         second(slice(half * 256, half * 256 + 256), 1, factor, delta)
-        for s in (2, 1, 3):
+        for s in (1, 2, 3):
             at = key_slot(s, half * 4) * 16
-            x_out[s - 1, half] = dkeys[at : at + 64, :].astype(jnp.bfloat16)
-            copy = remote(
-                x_out.at[s - 1, half], x_in.at[s - 1, half], s_x.at[s - 1, half], r_x.at[s - 1, half], xdev(s)
-            )
-            copy.start()
-            x_sends.append(copy)
+            x_out[s - 1, half * 64 : half * 64 + 64, :] = dkeys[at : at + 64, :].astype(jnp.bfloat16)
+        for j in LEAVE[half * 4 : half * 4 + 4]:
+            for s in (2, 1, 3):
+                x_send(s, j).start()
 
     core_sends = []
     hops_y = (2, 1, 3, 0)
@@ -285,22 +298,23 @@
     def z_send(j):
         return remote(kslot(z_out, j), z_in.at[z], s_z.at[j], r_z.at[z], dev(z_=zmod(HOPS[j] - parity)))
 
-    def sum_x(half):
-        at = key_slot(0, half * 4) * 16
-        mine = dkeys[at : at + 64, :]
-        for i, s in enumerate((2, 1, 3)):
-            x_sends[half * 3 + i].wait_recv()
-            mine = mine + x_in[s - 1, half].astype(jnp.float32)
-        dkeys[at : at + 64, :] = mine
-        z_out[half * 64 : half * 64 + 64, :] = mine.astype(jnp.bfloat16)
-        for j in ((1, 2, 0, 3), (7, 4, 6, 5))[half]:
-            if j == OWN:
-                pl.when(parity == 1)(lambda: z_send(OWN).start())
-            else:
-                z_send(j).start()
+    def sum_x(j):
+        at = key_slot(0, j) * 16
+        mine = dkeys[at : at + 16, :]
+        for s in (1, 3, 2):
+            x_send(s, j).wait_recv()
+            mine = mine + x_in[s - 1, j * 16 : j * 16 + 16, :].astype(jnp.float32)
+        dkeys[at : at + 16, :] = mine
+        z_out[j * 16 : j * 16 + 16, :] = mine.astype(jnp.bfloat16)
+        if j == OWN:
+            pl.when(parity == 1)(lambda: z_send(OWN).start())
+        else:
+            z_send(j).start()
 
     for at in range(4):
         query_part(at)
+    for j in LEAVE[:4]:
+        sum_x(j)
     dq_sends = []
     for at, s in enumerate(hops_y[:3]):
         core_sends[at].wait_recv()
@@ -308,8 +322,8 @@
         copy = remote(dq_out.at[at], dq_in.at[at], s_dq.at[at], r_dq.at[at], dev(y_=ymod(s)))
         copy.start()
         dq_sends.append(copy)
-    sum_x(0)
-    sum_x(1)
+    for j in LEAVE[4:]:
+        sum_x(j)
 
     fin = [dev(xh_=1 - xh, y_=ymod(s)) for s in (2, 1, 3, 0)] + [dev(y_=ymod(s)) for s in (2, 1, 3)]
 
@@ -359,11 +373,12 @@
 
     for i in range(4):
         fin_send(g, 7 + i, core).wait_send()
-    for copy in row_sends + stat_sends + core_sends + x_sends + dq_sends:
+    for copy in row_sends + stat_sends + core_sends + dq_sends:
         copy.wait_send()
     for j in range(8):
         for s in (2, 1, 3):
             forward(j, s).wait_send()
+            x_send(s, j).wait_send()
         if j == OWN:
             pl.when(parity == 1)(lambda: z_send(OWN).wait_send())
         else:
@@ -396,8 +411,8 @@
             pltpu.VMEM((4, 128, WIDTH), f32),
             pltpu.VMEM((3, 128, WIDTH), bf16),
             pltpu.VMEM((3, 128, WIDTH), bf16),
-            pltpu.VMEM((3, 2, 64, WIDTH), bf16),
-            pltpu.VMEM((3, 2, 64, WIDTH), bf16),
+            pltpu.VMEM((3, 128, WIDTH), bf16),
+            pltpu.VMEM((3, 128, WIDTH), bf16),
             pltpu.VMEM((128, WIDTH), bf16),
             pltpu.VMEM((16, 16, WIDTH), bf16),
             pltpu.VMEM((128, WIDTH), bf16),
@@ -405,7 +420,7 @@
             dma((16,)), dma((8,)), dma((8, 3)), dma((4, 8)),
             dma((2, 8)), dma((2, 8)),
             dma((4,)), dma((4,)), dma((3,)), dma((3,)),
-            dma((3, 2)), dma((3, 2)), dma((8,)), dma((16,)),
+            dma((3, 8)), dma((3, 8)), dma((8,)), dma((16,)),
             dma((11,)), dma((8,)),
         ],
         compiler_params=pltpu.CompilerParams(

time: 70.2 us -> 66.7 us (0.950)
  Pallas kernels: 66.1 us -> 62.6 us
    pallas_call x1, Pallas kernels: 66.1 us -> 62.6 us  [on_device(): pl.pallas_call(kernel, out_shape=(jax.ShapeDtypeStruct((128, WIDTH), bf16...]
where the time goes in v3:
time: 66.7 us; the launch traced here: 66.6 us
  Pallas kernels  62.6 us (94%)
  local copies, waits for them, and re-layouts  2.64 us (4%)
  between operations  1.35 us (2%)
    pallas_call x1, Pallas kernels, on_device(): pl.pallas_call(kernel, out_shape=(jax.ShapeDtypeStruct((128, WIDTH), bf16...  62.6 us
    unnamed x7, local copies, waits for them, and re-layouts  2.64 us

profile of v3, /device:TPU:1, one launch (start us, length us, event | category | flops | bytes accessed | tf_op | source)
XLA Modules:
  0.0 66.6 jit_solution(7107453055145726089)
XLA Ops:
  0.6 0.0 copy-start
  1.3 0.0 copy-start.1
  1.3 1.1 %copy.6.cache_ref = bf16[128,576]{1,0:T(8,128)(2,1)S(1)} copy(bf16[128,576]{0,1:T(8,128)(2,1)} %param.6) | data formatting | bytes 294912 | tf_op args[2]
  2.4 0.0 copy-done
  2.4 0.0 copy-done.1
  2.4 62.6 %latent_attention_backward.1 = (bf16[128,576]{1,0:T(8,128)(2,1)S(1)}, f32[128,576]{1,0:T(8,128)S(1)}) custom-call(s32[1]{0:T(128)S(6)} %copy.9.start_ref, bf16[128,576]{1,0:T(8,128)(2,1)S(1)} %bitcast.4, bf16[128,512]{1,0:T(8,128)(2,1)S(1)} %bitcast.5, bf16[128,576]{1,0:T(8,128)(2,1)S(1)} %copy.6.cache_ref), custom_call_target="tpu_custom_call" | custom-call | flops 2886000128 | bytes 900000 | tf_op jit(solution)/shard_map/latent_attention_backward/pallas_call | solution.py:392
  65.0 0.9 %copy.7 = f32[128,576]{0,1:T(8,128)} copy(f32[128,576]{1,0:T(8,128)S(1)} %get-tuple-element.7) | data formatting | bytes 589824
  65.9 0.7 %copy.10 = bf16[16,8,576]{2,1,0:T(8,128)(2,1)} copy(bf16[16,8,576]{2,1,0:T(8,128)(2,1)S(1)} %bitcast.3) | data formatting | bytes 294912
Async XLA Ops:
  0.6 1.8 %copy-start = (bf16[16,8,576]{2,1,0:T(8,128)(2,1)S(1)}, bf16[16,8,576]{2,1,0:T(8,128)(2,1)}, u32[]{:S(2)}) copy-start(bf16[16,8,576]{2,1,0:T(8,128)(2,1)} %param.4) | copy-start | bytes 442372
  1.3 1.1 %copy-start.1 = (bf16[16,8,512]{2,1,0:T(8,128)(2,1)S(1)}, bf16[16,8,512]{2,1,0:T(8,128)(2,1)}, u32[]{:S(2)}) copy-start(bf16[16,8,512]{2,1,0:T(8,128)(2,1)} %param.5) | copy-start | bytes 393220

commit v4 on v3

--- a/solution.py
+++ b/solution.py
@@ -26,7 +26,7 @@
     start_ref, query_ref, cotan_ref, cache_ref,
     dq_ref, dc_ref,
     rows_q, rows_g, keys, probs, gprobs, gscores, plow, dkeys, stats,
-    dq_part, dq_core, dq_out, dq_in, x_out, x_in, z_out, z_in, done,
+    dq_part, dq_core, dq_out, dq_in, x_out, x_in, z_out, z_in,
     s_rows, r_q, r_g, s_key, r_zkey, s_fwd, r_xkey, s_stat, r_stat,
     s_core, r_core, s_dq, r_dq, s_x, r_x, s_z, r_z, s_fin, r_fin,
 ):
@@ -328,7 +328,7 @@
     fin = [dev(xh_=1 - xh, y_=ymod(s)) for s in (2, 1, 3, 0)] + [dev(y_=ymod(s)) for s in (2, 1, 3)]
 
     def fin_send(slot, i, to):
-        return remote(kslot(done, slot), kslot(done, slot), s_fin.at[i], r_fin.at[slot], to)
+        return remote(kslot(dc_ref, slot), kslot(dc_ref, slot), s_fin.at[i], r_fin.at[slot], to)
 
     def wait_fin(slot):
         fin_send(slot, 0, core).wait_recv()
@@ -341,7 +341,7 @@
             zz = zmod(s)
             remote(kslot(z_out, 0), z_in.at[zz], s_z.at[0], r_z.at[zz], core).wait_recv()
             acc = acc + z_in[zz].astype(jnp.float32)
-        done[pl.ds(pl.multiple_of(g * 16, 16), 16), :] = acc.astype(jnp.bfloat16)
+        dc_ref[pl.ds(pl.multiple_of(g * 16, 16), 16), :] = acc.astype(jnp.bfloat16)
         for i, to in enumerate(fin):
             fin_send(g, i, to).start()
 
@@ -362,7 +362,6 @@
         fin_send(slot, 7 + i, core).start()
     for s in (0, 1, 3, 2):
         wait_fin(ymod(s) * 2 + 1 - k)
-    dc_ref[...] = done[...].astype(jnp.float32)
 
     @pl.when(parity == 0)
     def _():
@@ -393,7 +392,7 @@
         kernel,
         out_shape=(
             jax.ShapeDtypeStruct((128, WIDTH), bf16),
-            jax.ShapeDtypeStruct((128, WIDTH), f32),
+            jax.ShapeDtypeStruct((128, WIDTH), bf16),
         ),
         in_specs=[pl.BlockSpec(memory_space=pltpu.SMEM), vmem, vmem, vmem],
         out_specs=[vmem, vmem],
@@ -415,7 +414,6 @@
             pltpu.VMEM((3, 128, WIDTH), bf16),
             pltpu.VMEM((128, WIDTH), bf16),
             pltpu.VMEM((16, 16, WIDTH), bf16),
-            pltpu.VMEM((128, WIDTH), bf16),
             dma((14,)), dma((8,)), dma((8,)),
             dma((16,)), dma((8,)), dma((8, 3)), dma((4, 8)),
             dma((2, 8)), dma((2, 8)),
@@ -434,7 +432,7 @@
         grad_out.reshape(128, LATENT),
         latent_cache,
     )
-    return query_grad.reshape(queries.shape), cache_grad
+    return query_grad.reshape(queries.shape), cache_grad.astype(f32)
 
 
 def solution(mesh):

time: 66.7 us -> 66.7 us (level)
  no operation moved by 1% of the time
where the time goes in v4:
time: 66.7 us; the launch traced here: 66.5 us
  Pallas kernels  62.5 us (94%)
  local copies, waits for them, and re-layouts  2.61 us (4%)
  between operations  1.35 us (2%)
    pallas_call x1, Pallas kernels, on_device(): pl.pallas_call(kernel, out_shape=(jax.ShapeDtypeStruct((128, WIDTH), bf16...  62.5 us
    unnamed x7, local copies, waits for them, and re-layouts  2.61 us

profile of v4, /device:TPU:1, one launch (start us, length us, event | category | flops | bytes accessed | tf_op | source)
XLA Modules:
  0.0 66.5 jit_solution(17959775261906075668)
XLA Ops:
  0.6 0.0 copy-start
  1.3 0.0 copy-start.1
  1.3 1.1 %copy.6.cache_ref = bf16[128,576]{1,0:T(8,128)(2,1)S(1)} copy(bf16[128,576]{0,1:T(8,128)(2,1)} %param.6) | data formatting | bytes 294912 | tf_op args[2]
  2.4 0.0 copy-done
  2.4 0.0 copy-done.1
  2.4 62.5 %latent_attention_backward.1 = (bf16[128,576]{1,0:T(8,128)(2,1)S(1)}, bf16[128,576]{1,0:T(8,128)(2,1)S(1)}) custom-call(s32[1]{0:T(128)S(6)} %copy.9.start_ref, bf16[128,576]{1,0:T(8,128)(2,1)S(1)} %bitcast.4, bf16[128,512]{1,0:T(8,128)(2,1)S(1)} %bitcast.5, bf16[128,576]{1,0:T(8,128)(2,1)S(1)} %copy.6.cache_ref), custom_call_target="tpu_custom_call" | custom-call | flops 2886000128 | bytes 900000 | tf_op jit(solution)/shard_map/latent_attention_backward/pallas_call | solution.py:391
  65.0 0.8 %copy.7 = f32[128,576]{0,1:T(8,128)} copy(bf16[128,576]{1,0:T(8,128)(2,1)S(1)} %get-tuple-element.5) | data formatting | bytes 442368
  65.8 0.7 %copy.10 = bf16[16,8,576]{2,1,0:T(8,128)(2,1)} copy(bf16[16,8,576]{2,1,0:T(8,128)(2,1)S(1)} %bitcast.3) | data formatting | bytes 294912
Async XLA Ops:
  0.6 1.8 %copy-start = (bf16[16,8,576]{2,1,0:T(8,128)(2,1)S(1)}, bf16[16,8,576]{2,1,0:T(8,128)(2,1)}, u32[]{:S(2)}) copy-start(bf16[16,8,576]{2,1,0:T(8,128)(2,1)} %param.4) | copy-start | bytes 442372
  1.3 1.1 %copy-start.1 = (bf16[16,8,512]{2,1,0:T(8,128)(2,1)S(1)}, bf16[16,8,512]{2,1,0:T(8,128)(2,1)}, u32[]{:S(2)}) copy-start(bf16[16,8,512]{2,1,0:T(8,128)(2,1)} %param.5) | copy-start | bytes 393220
